TPU v7x, 32 devices: a whole 2x2x4 slice. The times are simulated.
32 devices in a mesh: seq: 8 (over y, x, core), batch: 4 (over z).
Axes of the slice: x: 2, y: 2, z: 4, core: 2. Of those that a mesh axis runs over, the one named last changes fastest.
Arguments:
- tokens: bfloat16 [16, 1024, 768], P('batch', 'seq'), may hold values from -6 to 6
- first_gain: float32 [768], replicated, may hold values from 0.25 to 1.75
- first_shift: float32 [768], replicated, may hold values from -1.75 to 1.75
- mixer_input: bfloat16 [768, 2304], replicated, may hold values from -0.21875 to 0.21875
- conv_kernel: bfloat16 [256, 768], replicated, may hold values from -0.375 to 0.375
- mixer_output: bfloat16 [768, 768], replicated, may hold values from -0.375 to 0.375
- second_gain: float32 [768], replicated, may hold values from 0.25 to 1.75
- second_shift: float32 [768], replicated, may hold values from -1.75 to 1.75
- widen_weight: bfloat16 [768, 3072], replicated, may hold values from -0.21875 to 0.21875
- narrow_weight: bfloat16 [3072, 768], replicated, may hold values from -0.15625 to 0.15625
- cotangent: bfloat16 [16, 1024, 768], P('batch', 'seq'), may hold values from -6 to 6
Outputs:
- block_output: bfloat16 [16, 1024, 768], P('batch', 'seq')
- grad_tokens: bfloat16 [16, 1024, 768], P('batch', 'seq')
- grad_first_gain: float32 [768], P('seq')
- grad_first_shift: float32 [768], P('seq')
- grad_mixer_input: float32 [768, 2304], P('seq')
- grad_conv_kernel: float32 [256, 768], P('seq')
- grad_mixer_output: float32 [768, 768], P('seq')
- grad_second_gain: float32 [768], P('seq')
- grad_second_shift: float32 [768], P('seq')
- grad_widen: float32 [768, 3072], P('seq')
- grad_narrow: float32 [3072, 768], P('seq')
All inputs are finite; a program needn't handle non-finite values.
Results may differ from a plain program's by a relative error of at most 0.0085.
Values sent between devices are 32-bit elements; how exact they have to be, the bound alone decides.
No kernel may reach another device: no remote copies, remote signals or barrier semaphores. Data moves between devices by JAX's collectives and lax.ppermute only.
A program may use at most 192 MiB of HBM per device.

v0:
```python
import math

import jax
import jax.numpy as jnp
from jax import lax
from jax.sharding import PartitionSpec as P

norm_epsilon = 1e-05
shrink_level = 0.003
highest = lax.Precision.HIGHEST


def norm_apply(values, scale_row, shift_row):
    centered = values - jnp.mean(values, axis=-1, keepdims=True)
    inverse = lax.rsqrt(jnp.mean(centered * centered, axis=-1, keepdims=True) + norm_epsilon)
    return centered * inverse * scale_row + shift_row


def shape_kernel(raw_kernel):
    shrunk = raw_kernel - shrink_level * jnp.tanh(raw_kernel / shrink_level)
    padded = jnp.pad(shrunk, ((1, 1), (0, 0)))
    return (padded[:-2] + padded[1:-1] + padded[2:]) / 3.0


def exact_gelu(values):
    return 0.5 * values * (1.0 + lax.erf(values / math.sqrt(2.0)))


def angle_table(leading, trailing, modulus):
    product = leading[:, None] * trailing[None, :] % modulus
    return 2.0 * math.pi / modulus * product.astype(jnp.float32)


def index_range(length):
    return jnp.arange(length, dtype=jnp.int32)


def complex_times(former, latter):
    return jnp.stack(
        [
            former[0] * latter[0] - former[1] * latter[1],
            former[0] * latter[1] + former[1] * latter[0],
        ]
    )


def times_conjugate(former, latter):
    return jnp.stack(
        [
            former[0] * latter[0] + former[1] * latter[1],
            former[1] * latter[0] - former[0] * latter[1],
        ]
    )


def spread_forward(signal, axis_count, device):
    seqs_here, local_len, features = signal.shape
    shard_cells = local_len // axis_count
    total_len = 2 * axis_count * local_len
    blocks = lax.all_to_all(
        signal.reshape(seqs_here, 1, local_len, features),
        "seq",
        split_axis=2,
        concat_axis=1,
        tiled=True,
    )
    outer_angle = angle_table(index_range(2 * axis_count), index_range(axis_count), 2 * axis_count)
    real_part = jnp.einsum("ks,bscd->bkcd", jnp.cos(outer_angle), blocks, precision=highest)
    imag_part = -jnp.einsum("ks,bscd->bkcd", jnp.sin(outer_angle), blocks, precision=highest)
    cell_index = device * shard_cells + index_range(shard_cells)
    twist_angle = angle_table(index_range(2 * axis_count), cell_index, total_len)[None, :, :, None]
    twist_cos = jnp.cos(twist_angle)
    twist_sin = jnp.sin(twist_angle)
    turned = jnp.stack(
        [
            real_part * twist_cos + imag_part * twist_sin,
            imag_part * twist_cos - real_part * twist_sin,
        ]
    )
    owned = lax.all_to_all(turned, "seq", split_axis=2, concat_axis=3, tiled=True)
    inner_angle = angle_table(index_range(local_len), index_range(local_len), local_len)
    cosine_table = jnp.cos(inner_angle)
    sine_table = jnp.sin(inner_angle)
    spec_real = jnp.einsum("qc,bjcd->bjqd", cosine_table, owned[0], precision=highest) + jnp.einsum(
        "qc,bjcd->bjqd", sine_table, owned[1], precision=highest
    )
    spec_imag = jnp.einsum("qc,bjcd->bjqd", cosine_table, owned[1], precision=highest) - jnp.einsum(
        "qc,bjcd->bjqd", sine_table, owned[0], precision=highest
    )
    return jnp.stack([spec_real, spec_imag])


def spread_inverse(spectrum, axis_count, device):
    seqs_here = spectrum.shape[1]
    pair_count = spectrum.shape[2]
    local_len = spectrum.shape[3]
    features = spectrum.shape[4]
    total_len = 2 * axis_count * local_len
    inner_angle = angle_table(index_range(local_len), index_range(local_len), local_len)
    cosine_table = jnp.cos(inner_angle)
    sine_table = jnp.sin(inner_angle)
    part_real = jnp.einsum(
        "cq,bjqd->bjcd", cosine_table, spectrum[0], precision=highest
    ) - jnp.einsum("cq,bjqd->bjcd", sine_table, spectrum[1], precision=highest)
    part_imag = jnp.einsum(
        "cq,bjqd->bjcd", cosine_table, spectrum[1], precision=highest
    ) + jnp.einsum("cq,bjqd->bjcd", sine_table, spectrum[0], precision=highest)
    outer_index = device * pair_count + index_range(pair_count)
    twist_angle = angle_table(outer_index, index_range(local_len), total_len)[None, :, :, None]
    twist_cos = jnp.cos(twist_angle)
    twist_sin = jnp.sin(twist_angle)
    turned = jnp.stack(
        [
            part_real * twist_cos - part_imag * twist_sin,
            part_imag * twist_cos + part_real * twist_sin,
        ]
    )
    spread = lax.all_to_all(turned, "seq", split_axis=3, concat_axis=2, tiled=True)
    back_angle = angle_table(index_range(axis_count), index_range(2 * axis_count), 2 * axis_count)
    result = (
        jnp.einsum("sk,bkcd->bscd", jnp.cos(back_angle), spread[0], precision=highest)
        - jnp.einsum("sk,bkcd->bscd", jnp.sin(back_angle), spread[1], precision=highest)
    ) / total_len
    arrived = lax.all_to_all(result, "seq", split_axis=1, concat_axis=2, tiled=True)
    return arrived.reshape(seqs_here, local_len, features)


def own_spectrum(kernel_taps, axis_count, device, local_len):
    tap_count, features = kernel_taps.shape
    freq_index = (
        (device * 2 + index_range(2))[:, None] + 2 * axis_count * index_range(local_len)[None, :]
    ).reshape(-1)
    angles = angle_table(index_range(tap_count), freq_index, 2 * axis_count * local_len)
    real_part = jnp.einsum("tf,td->fd", jnp.cos(angles), kernel_taps, precision=highest)
    imag_part = -jnp.einsum("tf,td->fd", jnp.sin(angles), kernel_taps, precision=highest)
    return jnp.stack([real_part, imag_part]).reshape(2, 2, local_len, features)


def on_device(
    tokens,
    first_gain,
    first_shift,
    mixer_input,
    conv_kernel,
    mixer_output,
    second_gain,
    second_shift,
    widen_weight,
    narrow_weight,
    cotangent,
):
    axis_count = lax.axis_size("seq")
    device = lax.axis_index("seq")
    seqs_here, local_len, features = tokens.shape
    row_total = seqs_here * local_len
    total_len = 2 * axis_count * local_len

    def to_spectrum(signal):
        return spread_forward(signal, axis_count, device)

    def from_spectrum(spectrum):
        return spread_inverse(spectrum, axis_count, device)

    def spectrum_of(kernel_taps):
        return own_spectrum(kernel_taps, axis_count, device, local_len)[:, None]

    flat_tokens = tokens.reshape(row_total, features).astype(jnp.float32)
    normed, first_pull = jax.vjp(norm_apply, flat_tokens, first_gain, first_shift)
    normed_low = normed.astype(jnp.bfloat16)
    mixed_rows = jnp.dot(normed_low, mixer_input, preferred_element_type=jnp.float32)
    query_rows = mixed_rows[:, :features]
    key_rows = mixed_rows[:, features : 2 * features]
    value_rows = mixed_rows[:, 2 * features :]
    kernel_taps, taps_pull = jax.vjp(shape_kernel, conv_kernel.astype(jnp.float32))
    kernel_spectrum, spectrum_pull = jax.vjp(spectrum_of, kernel_taps)
    product = (key_rows * value_rows).reshape(seqs_here, local_len, features)
    product_spectrum = to_spectrum(product)
    convolved = from_spectrum(complex_times(product_spectrum, kernel_spectrum)).reshape(
        row_total, features
    )
    gated_low = (query_rows * convolved).astype(jnp.bfloat16)
    branch = jnp.dot(gated_low, mixer_output, preferred_element_type=jnp.float32)
    middle = flat_tokens + branch
    second, second_pull = jax.vjp(norm_apply, middle, second_gain, second_shift)
    second_low = second.astype(jnp.bfloat16)
    hidden = jnp.dot(second_low, widen_weight, preferred_element_type=jnp.float32)
    active, active_pull = jax.vjp(exact_gelu, hidden)
    active_low = active.astype(jnp.bfloat16)
    feed_out = jnp.dot(active_low, narrow_weight, preferred_element_type=jnp.float32)
    block_output = (middle + feed_out).astype(jnp.bfloat16).reshape(tokens.shape)
    flat_cot = cotangent.reshape(row_total, features)
    grad_narrow = jnp.dot(active_low.T, flat_cot, preferred_element_type=jnp.float32)
    grad_active = jnp.dot(flat_cot, narrow_weight.T, preferred_element_type=jnp.float32)
    grad_hidden = active_pull(grad_active)[0].astype(jnp.bfloat16)
    grad_widen = jnp.dot(second_low.T, grad_hidden, preferred_element_type=jnp.float32)
    grad_second = jnp.dot(grad_hidden, widen_weight.T, preferred_element_type=jnp.float32)
    grad_middle, grad_second_gain, grad_second_shift = second_pull(grad_second)
    grad_middle = grad_middle + flat_cot.astype(jnp.float32)
    grad_branch = grad_middle.astype(jnp.bfloat16)
    grad_mixer_output = jnp.dot(gated_low.T, grad_branch, preferred_element_type=jnp.float32)
    grad_gated = jnp.dot(grad_branch, mixer_output.T, preferred_element_type=jnp.float32)
    grad_query = grad_gated * convolved
    grad_conv = (grad_gated * query_rows).reshape(seqs_here, local_len, features)
    grad_spectrum = to_spectrum(grad_conv)
    grad_product = from_spectrum(times_conjugate(grad_spectrum, kernel_spectrum)).reshape(
        row_total, features
    )
    cross_term = (
        jnp.sum(times_conjugate(grad_spectrum, product_spectrum), axis=1, keepdims=True) / total_len
    )
    grad_taps = spectrum_pull(cross_term)[0]
    grad_conv_kernel = taps_pull(grad_taps)[0]
    grad_mixed = jnp.concatenate(
        [grad_query, grad_product * value_rows, grad_product * key_rows], axis=1
    ).astype(jnp.bfloat16)
    grad_mixer_input = jnp.dot(normed_low.T, grad_mixed, preferred_element_type=jnp.float32)
    grad_normed = jnp.dot(grad_mixed, mixer_input.T, preferred_element_type=jnp.float32)
    grad_flat, grad_first_gain, grad_first_shift = first_pull(grad_normed)
    grad_tokens = (grad_middle + grad_flat).astype(jnp.bfloat16).reshape(tokens.shape)
    norm_grads = jnp.stack(
        [grad_first_gain, grad_first_shift, grad_second_gain, grad_second_shift], axis=1
    )
    row_input, row_kernel, row_output, row_widen, row_narrow, row_norms = (
        lax.psum_scatter(grad_mixer_input, "seq", scatter_dimension=0, tiled=True),
        lax.psum_scatter(grad_conv_kernel, "seq", scatter_dimension=0, tiled=True),
        lax.psum_scatter(grad_mixer_output, "seq", scatter_dimension=0, tiled=True),
        lax.psum_scatter(grad_widen, "seq", scatter_dimension=0, tiled=True),
        lax.psum_scatter(grad_narrow, "seq", scatter_dimension=0, tiled=True),
        lax.psum_scatter(norm_grads, "seq", scatter_dimension=0, tiled=True),
    )
    sum_input, sum_kernel, sum_output, sum_widen, sum_narrow, sum_norms = lax.psum(
        (row_input, row_kernel, row_output, row_widen, row_narrow, row_norms), "batch"
    )
    return (
        block_output,
        grad_tokens,
        sum_norms[:, 0],
        sum_norms[:, 1],
        sum_input,
        sum_kernel,
        sum_output,
        sum_norms[:, 2],
        sum_norms[:, 3],
        sum_widen,
        sum_narrow,
    )


def solution(mesh):
    in_specs = (
        P("batch", "seq", None),
        P(),
        P(),
        P(),
        P(),
        P(),
        P(),
        P(),
        P(),
        P(),
        P("batch", "seq", None),
    )
    out_specs = (
        P("batch", "seq", None),
        P("batch", "seq", None),
        P("seq"),
        P("seq"),
        P("seq", None),
        P("seq", None),
        P("seq", None),
        P("seq"),
        P("seq"),
        P("seq", None),
        P("seq", None),
    )
    return jax.shard_map(
        on_device, mesh=mesh, in_specs=in_specs, out_specs=out_specs, check_vma=False
    )
```

profile of v0, /device:TPU:0, one launch (start us, length us, event | category | flops | bytes accessed | tf_op | source)
XLA Modules:
  0.0 1031.7 jit_solution(818869358049246015)
XLA Ops:
  19.4 5.3 all-to-all-start
  24.9 20.8 %all-to-all-done = f32[4,1,128,768]{3,0,1,2:T(4,128)} async-done(((f32[4,1,128,768]{3,0,1,2:T(4,128)}), f32[4,1,128,768]{3,0,1,2:T(4,128)}, u32[]{:S(2)}, u32[]{:S(2)}) %all-to-all-start) | async-done | bytes 1572896 | tf_op jit(solution)/shard_map/all_to_all | solution.py:60
  50.9 4.3 fusion.13
  55.6 6.7 copy.94
  62.4 4.8 all-to-all-start.1
  74.9 4.8 convolution_negate_fusion
  83.3 55.5 %all-to-all-done.1 = f32[2,4,16,16,768]{4,3,1,0,2:T(8,128)} async-done(((f32[2,4,16,16,768]{4,3,1,0,2:T(8,128)}), f32[2,4,16,16,768]{4,3,1,0,2:T(8,128)}, u32[]{:S(2)}, u32[]{:S(2)}) %all-to-all-start.1) | async-done | bytes 6291488 | tf_op jit(solution)/shard_map/all_to_all | solution.py:80
  143.1 5.2 fusion.98
  148.6 5.4 fusion.96
  154.0 5.2 convolution_add_fusion.3
  159.3 5.6 convolution_subtract_fusion.3
  181.2 10.3 %copy.104 = f32[2,4,2,128,768]{4,2,1,0,3:T(2,128)} copy(f32[2,4,2,128,768]{3,4,2,1,0:T(8,128)} %pad_maximum_fusion.1) | data formatting | bytes 12582912 | tf_op jit(solution)/shard_map/stack | solution.py:112
  191.5 75.2 %all_to_all.102 = f32[2,4,2,128,768]{4,2,1,0,3:T(2,128)S(1)} all-to-all(f32[2,4,2,128,768]{4,2,1,0,3:T(2,128)} %copy.104), channel_id=1, replica_groups=mesh['seq'=8,'batch'=4] {'seq'}, dimensions={3} | all-to-all | bytes 12582912 | tf_op jit(solution)/shard_map/all_to_all | solution.py:118
  272.6 4.1 copy.106
  276.7 5.5 squeeze.50
  282.2 5.0 fusion.137
  287.2 4.1 copy.107
  291.3 5.3 squeeze.51
  296.6 4.4 multiply_bitcast_fusion.1
  301.5 24.1 %all_to_all.103 = f32[4,8,16,768]{3,2,0,1:T(8,128)S(1)} all-to-all(f32[4,8,16,768]{3,2,0,1:T(8,128)S(1)} %copy.108), channel_id=1, replica_groups=mesh['seq'=8,'batch'=4] {'seq'}, dimensions={1} | all-to-all | bytes 3145728 | tf_op jit(solution)/shard_map/all_to_all | solution.py:124
  331.2 6.5 add_convert_fusion
  337.7 5.4 multiply_reduce_fusion
  347.0 23.4 %all_to_all.104 = f32[4,1,128,768]{3,0,1,2:T(4,128)S(1)} all-to-all(f32[4,1,128,768]{3,0,1,2:T(4,128)S(1)} %copy.110), channel_id=1, replica_groups=mesh['seq'=8,'batch'=4] {'seq'}, dimensions={2} | all-to-all | bytes 3145728 | tf_op jit(solution)/shard_map/all_to_all | solution.py:60
  374.1 4.3 fusion.7
  378.9 6.7 copy.114
  385.6 4.8 all-to-all-start.5
  394.2 77.3 %all-to-all-done.5 = f32[2,4,16,16,768]{4,3,1,0,2:T(8,128)} async-done(((f32[2,4,16,16,768]{4,3,1,0,2:T(8,128)}), f32[2,4,16,16,768]{4,3,1,0,2:T(8,128)}, u32[]{:S(2)}, u32[]{:S(2)}) %all-to-all-start.5) | async-done | bytes 6291488 | tf_op jit(solution)/shard_map/all_to_all | solution.py:80
  475.9 5.2 fusion.92
  481.4 5.4 fusion.90
  486.8 5.2 convolution_add_fusion.1
  492.0 5.2 convolution_subtract_fusion.1
  516.2 8.9 fusion.285
  525.2 8.4 fusion.312
  534.1 5.7 fusion.67
  552.9 10.7 %copy.122 = f32[2,4,2,128,768]{4,2,1,0,3:T(2,128)} copy(f32[2,4,2,128,768]{3,4,2,1,0:T(8,128)} %pad_maximum_fusion.3) | data formatting | bytes 12582912 | tf_op jit(solution)/shard_map/stack | solution.py:112
  563.6 100.6 %all_to_all.105 = f32[2,4,2,128,768]{4,2,1,0,3:T(2,128)S(1)} all-to-all(f32[2,4,2,128,768]{4,2,1,0,3:T(2,128)} %copy.122), channel_id=1, replica_groups=mesh['seq'=8,'batch'=4] {'seq'}, dimensions={3} | all-to-all | bytes 12582912 | tf_op jit(solution)/shard_map/all_to_all | solution.py:118
  674.2 5.3 squeeze.54
  679.5 6.0 copy.125
  685.4 5.5 squeeze.55
  691.0 4.2 fusion.135
  697.6 29.8 %all_to_all.106 = f32[4,8,16,768]{3,2,0,1:T(8,128)S(1)} all-to-all(f32[4,8,16,768]{3,2,0,1:T(8,128)S(1)} %copy.126), channel_id=1, replica_groups=mesh['seq'=8,'batch'=4] {'seq'}, dimensions={1} | all-to-all | bytes 3145728 | tf_op jit(solution)/shard_map/all_to_all | solution.py:124
  729.5 5.0 fusion.41
  742.2 27.0 %reduce-scatter.17.cloned.1.call-done = f32[384,768]{1,0:T(8,128)} async-done(((f32[3072,768]{1,0:T(8,128)}), f32[384,768]{1,0:T(8,128)}) %reduce-scatter.17.cloned.1.call-update) | async-done | bytes 1179664 | tf_op jit(solution)/shard_map/reduce_scatter | solution.py:228
  769.2 69.3 %reduce-scatter.9.cloned.1.call-done = f32[96,2304]{1,0:T(8,128)} async-done(((f32[768,2304]{1,0:T(8,128)}), f32[96,2304]{1,0:T(8,128)}) %reduce-scatter.9.cloned.1.call-update) | async-done | bytes 884752 | tf_op jit(solution)/shard_map/reduce_scatter | solution.py:224
  838.6 7.4 add_convert_fusion.2
  847.7 28.2 %reduce-scatter.19.cloned.1.call-done = f32[96,4]{1,0:T(8,128)} async-done(((f32[768,4]{1,0:T(8,128)}), f32[96,4]{1,0:T(8,128)}) %reduce-scatter.19.cloned.1.call-update) | async-done | bytes 1552
  876.7 11.8 %psum.42 = f32[96,4]{0,1:T(4,128)S(1)} all-reduce(f32[96,4]{0,1:T(4,128)S(1)} %copy.145), channel_id=1, replica_groups=mesh['seq'=8,'batch'=4] {'batch'}, use_global_device_ids=true, to_apply=%region_13.14 | all-reduce | flops 384 | bytes 3072 | tf_op jit(solution)/shard_map/psum | solution.py:231
  889.0 128.0 %all-reduce.7.cloned.1.call-done = (f32[96,2304]{1,0:T(8,128)}, f32[32,768]{1,0:T(8,128)}, f32[96,768]{1,0:T(8,128)}, f32[96,3072]{1,0:T(8,128)}, f32[384,768]{1,0:T(8,128)}) async-done(((f32[96,2304]{1,0:T(8,128)}, f32[32,768]{1,0:T(8,128)}, f32[96,768]{1,0:T(8,128)}, f32[96,3072]{1,0:T(8,128)}, f32[384,768]{1,0:T(8,128)}), (f32[96,2304]{1,0:T(8,128)}, f32[32,768]{1,0:T(8,128)}, f32[96,768]{1,0:T(8,128)}, ...) | async-done | bytes 3637264 | tf_op jit(solution)/shard_map/psum | solution.py:231
  (265 shorter events, 143.0 us)
Async XLA Ops:
  7.2 5.7 copy-start
  19.4 26.3 %all-to-all-start = ((f32[4,1,128,768]{3,0,1,2:T(4,128)}), f32[4,1,128,768]{3,0,1,2:T(4,128)}, u32[]{:S(2)}, u32[]{:S(2)}) async-start(f32[4,1,128,768]{3,0,1,2:T(4,128)} %copy.90), calls=%async_computation | async-start | bytes 3145728 | tf_op jit(solution)/shard_map/all_to_all | solution.py:60
  62.4 76.4 %all-to-all-start.1 = ((f32[2,4,16,16,768]{4,3,1,0,2:T(8,128)}), f32[2,4,16,16,768]{4,3,1,0,2:T(8,128)}, u32[]{:S(2)}, u32[]{:S(2)}) async-start(f32[2,4,16,16,768]{4,3,1,0,2:T(8,128)} %copy.94), calls=%async_computation.1 | async-start | bytes 12582912 | tf_op jit(solution)/shard_map/all_to_all | solution.py:80
  67.8 4.9 copy-start.53
  159.2 15.1 %copy-start.1 = (f32[4,2,768,128]{3,2,1,0:T(8,128)}, f32[4,2,768,128]{3,2,1,0:T(8,128)S(1)}, u32[]{:S(2)}) copy-start(f32[4,2,768,128]{3,2,1,0:T(8,128)S(1)} %convolution_add_fusion.3) | copy-start | bytes 9437188
  159.3 5.6 copy-start.9
  159.3 5.6 copy-start.11
  164.9 9.5 copy-start.3
  282.2 5.1 copy-start.20
  296.6 29.1 %slice-start = ((s8[4718592]{0:T(1024)(128)(4,1)}), s8[4194304]{0:T(1024)(128)(4,1)S(1)}, s32[]{:S(2)}) async-start(s8[4718592]{0:T(1024)(128)(4,1)} %bitcast.358), calls=%async_computation.21 | async-start | bytes 8388608
  301.0 24.8 %slice-start.1 = ((s8[4718592]{0:T(1024)(128)(4,1)}), s8[524288]{0:T(1024)(128)(4,1)S(1)}, s32[]{:S(2)}) async-start(s8[4718592]{0:T(1024)(128)(4,1)} %bitcast.358), calls=%async_computation.22 | async-start | bytes 1048576
  301.5 26.9 %slice-start.4 = ((s8[4718592]{0:T(1024)(128)(4,1)}), s8[4194304]{0:T(1024)(128)(4,1)S(1)}, s32[]{:S(2)}) async-start(s8[4718592]{0:T(1024)(128)(4,1)} %bitcast.375), calls=%async_computation.25 | async-start | bytes 8388608
  328.0 15.2 %copy-start.22 = (f32[512,768]{1,0:T(8,128)}, f32[512,768]{1,0:T(8,128)S(1)}, u32[]{:S(2)}) copy-start(f32[512,768]{1,0:T(8,128)S(1)} %get-tuple-element.61) | copy-start | bytes 4718596
  328.0 15.2 %copy-start.47 = (f32[512]{0:T(512)}, f32[512]{0:T(512)S(1)}, u32[]{:S(2)}) copy-start(f32[512]{0:T(512)S(1)} %broadcast_multiply_fusion.1) | copy-start | bytes 6148
  328.4 14.8 %copy-start.59 = (f32[512]{0:T(512)}, f32[512]{0:T(512)S(1)}, u32[]{:S(2)}) copy-start(f32[512]{0:T(512)S(1)} %fusion.163) | copy-start | bytes 6148
  385.6 85.9 %all-to-all-start.5 = ((f32[2,4,16,16,768]{4,3,1,0,2:T(8,128)}), f32[2,4,16,16,768]{4,3,1,0,2:T(8,128)}, u32[]{:S(2)}, u32[]{:S(2)}) async-start(f32[2,4,16,16,768]{4,3,1,0,2:T(8,128)} %copy.114), calls=%async_computation.5 | async-start | bytes 12582912 | tf_op jit(solution)/shard_map/all_to_all | solution.py:80
  390.4 351.7 %reduce-scatter.13.cloned.1.call-start = ((), (), s32[]{:S(2)}) async-start(), calls=%async_computation.16 | async-start | bytes 2654208 | tf_op jit(solution)/shard_map/reduce_scatter | solution.py:226
  394.1 348.0 %reduce-scatter.11.cloned.1.call-start = ((), (), s32[]{:S(2)}) async-start(), calls=%async_computation.15 | async-start | bytes 884736 | tf_op jit(solution)/shard_map/reduce_scatter | solution.py:225
  492.0 5.2 copy-start.5
  492.0 5.2 copy-start.2
  492.0 5.2 copy-start.4
  502.9 5.9 copy-start.54
  508.8 6.0 copy-start.28
  508.8 7.4 copy-start.48
  508.8 7.4 copy-start.60
  508.8 7.4 copy-start.65
  516.1 226.0 %reduce-scatter.15.cloned.1.call-start = ((), (), s32[]{:S(2)}) async-start(), calls=%async_computation.17 | async-start | bytes 10616832 | tf_op jit(solution)/shard_map/reduce_scatter | solution.py:227
  525.2 244.0 %reduce-scatter.17.cloned.1.call-start = ((), (), s32[]{:S(2)}) async-start(), calls=%async_computation.18 | async-start | bytes 10616832 | tf_op jit(solution)/shard_map/reduce_scatter | solution.py:228
  533.7 304.9 %reduce-scatter.9.cloned.1.call-start = ((), (), s32[]{:S(2)}) async-start(), calls=%async_computation.14 | async-start | bytes 7962624 | tf_op jit(solution)/shard_map/reduce_scatter | solution.py:224
  534.1 5.7 copy-start.6
  534.1 5.7 copy-start.8
  534.1 5.7 copy-start.10
  534.1 5.7 copy-start.12
  695.2 32.3 %slice-start.2 = ((s8[4718592]{0:T(1024)(128)(4,1)}), s8[4194304]{0:T(1024)(128)(4,1)S(1)}, s32[]{:S(2)}) async-start(s8[4718592]{0:T(1024)(128)(4,1)} %bitcast.360), calls=%async_computation.23 | async-start | bytes 8388608
  697.1 30.4 %slice-start.3 = ((s8[4718592]{0:T(1024)(128)(4,1)}), s8[524288]{0:T(1024)(128)(4,1)S(1)}, s32[]{:S(2)}) async-start(s8[4718592]{0:T(1024)(128)(4,1)} %bitcast.360), calls=%async_computation.24 | async-start | bytes 1048576
  734.5 141.4 %reduce-scatter.19.cloned.1.call-start = ((), (), s32[]{:S(2)}) async-start(), calls=%async_computation.19 | async-start | bytes 442368
  741.8 275.3 %all-reduce.7.cloned.1.call-start = ((), (), s32[]{:S(2)}) async-start(), calls=%async_computation.20 | async-start | bytes 7274496 | tf_op jit(solution)/shard_map/psum | solution.py:231
  838.5 7.5 copy-start.61
  838.5 7.5 copy-start.15
  838.6 7.4 copy-start.18
  838.6 7.4 copy-start.24
  838.6 7.4 copy-start.27
  838.6 7.4 copy-start.41
  838.6 7.4 copy-start.44
  838.6 7.4 copy-start.46
  838.6 7.4 copy-start.52
  1017.0 5.5 copy-start.31
  1017.0 6.5 copy-start.30
  (38 other events, 76.7 us)
Sparse Core Ops, SparseCore 0:
  394.6 62.2 reduce-scatter.12
  516.3 34.8 reduce-scatter.10
  555.1 127.3 reduce-scatter.14
  686.2 82.9 reduce-scatter.16
  773.0 65.4 reduce-scatter.8
  842.0 33.8 reduce-scatter.18
  878.6 138.3 all-reduce.6
where the time goes:
time: 1040 us; the launch traced here: 1030 us
  waiting for transfers between devices  406 us (39%)
  blocking collectives  265 us (25%)
  matrix products  172 us (17%)
  local copies, waits for them, and re-layouts  129 us (12%)
  other arithmetic  27.5 us (3%)
  starting transfers between devices  15.8 us (2%)
  between operations  15.8 us (2%)
    all_to_all x2, blocking collectives, spread_inverse(): lax.all_to_all(turned, 'seq', split_axis=3, concat_axis=2, tiled=True)  176 us
    all_to_all x2, waiting for transfers between devices, spread_forward(): lax.all_to_all(turned, 'seq', split_axis=2, concat_axis=3, tiled=True)  133 us
    psum x1, waiting for transfers between devices, on_device(): lax.psum((row_input, row_kernel, row_output, row_widen, row_narrow, row_n...  128 us
    reduce_scatter x1, waiting for transfers between devices, on_device(): lax.psum_scatter(grad_mixer_input, 'seq', scatter_dimension=0, tiled=True)  69.3 us
    all_to_all x2, blocking collectives, spread_inverse(): lax.all_to_all(result, 'seq', split_axis=1, concat_axis=2, tiled=True)  53.9 us
    unnamed x8, waiting for transfers between devices  28.3 us
    reduce_scatter x1, waiting for transfers between devices, on_device(): lax.psum_scatter(grad_narrow, 'seq', scatter_dimension=0, tiled=True)  27 us
    all_to_all x1, blocking collectives, spread_forward(): lax.all_to_all(signal.reshape(seqs_here, 1, local_len, features), 'seq',...  23.4 us
  transfers between devices with their start and end apart: 10, of which 7 were waited for; matrix products, arithmetic and copies ran while one was open for 16% of the time, Pallas kernels for 0%

commit v1 on v0

v1 whole, which is shorter than its diff:
```python
import functools
import math

import jax
import jax.numpy as jnp
import numpy as np
from jax import lax
from jax.experimental import pallas as pl
from jax.experimental.pallas import tpu as pltpu
from jax.sharding import PartitionSpec as P

norm_epsilon = 1e-05
shrink_level = 0.003
highest = lax.Precision.HIGHEST
low_type = jnp.bfloat16


def split_low(table):
    high = table.astype(np.float32).astype(jnp.bfloat16)
    rest = (table - high.astype(np.float64)).astype(np.float32).astype(jnp.bfloat16)
    return high, rest


@functools.lru_cache(maxsize=None)
def half_tables(block):
    order = np.concatenate([np.arange(0, block, 2), np.arange(1, block, 2)])
    theta = np.pi * (2 * order + 1) / (2 * block)
    place = np.arange(block)
    early = theta[:, None] * place[None, :]
    late = theta[None, :] * (block + place[:, None])
    forward = np.concatenate([np.cos(early), -np.sin(early)], axis=0)
    inverse = np.concatenate([np.cos(late), -np.sin(late)], axis=1) / block
    return forward, inverse


def stacked_pair(table):
    high, rest = split_low(table)
    return np.concatenate([high, rest], axis=1)


def turn(spectrum, block):
    half = block // 2
    real, imag = spectrum[:block], spectrum[block:]
    return jnp.concatenate([imag[:half], -imag[half:], -real[:half], real[half:]], axis=0)


def turn_back(spectrum, block):
    half = block // 2
    first, last = spectrum[:block], spectrum[block:]
    return jnp.concatenate([-last[:half], last[half:], first[:half], -first[half:]], axis=0)


def twice(values):
    rounded = values.astype(low_type)
    return jnp.concatenate([rounded, rounded], axis=0)


def low_dot(left, right):
    return jnp.dot(left, right, preferred_element_type=jnp.float32)


def convolve_kernel(count, block, table_ref, high_ref, rest_ref, filter_ref, query_ref, *refs):
    block_refs, (convolved_ref, gated_ref) = refs[:count], refs[count:]
    real, imag = 0.0, 0.0
    for place in range(count):
        spectrum = low_dot(table_ref[...], twice(block_refs[place][0]))
        own_real, own_imag = spectrum[:block], spectrum[block:]
        filter_real = filter_ref[place, :block, :]
        filter_imag = filter_ref[place, block:, :]
        real += own_real * filter_real - own_imag * filter_imag
        imag += own_real * filter_imag + own_imag * filter_real
    total = jnp.concatenate([real, imag], axis=0).astype(low_type)
    convolved = low_dot(high_ref[...], total) + low_dot(rest_ref[...], total)
    convolved_ref[0] = convolved
    gated_ref[0] = (query_ref[0] * convolved).astype(low_type)


def pull_kernel(count, block, table_ref, high_ref, rest_ref, filter_ref, key_ref, value_ref, *refs):
    block_refs, (key_out_ref, value_out_ref) = refs[:count], refs[count:]
    real, imag = 0.0, 0.0
    for place in range(count):
        spectrum = low_dot(table_ref[...], twice(block_refs[place][0]))
        own_real, own_imag = spectrum[:block], spectrum[block:]
        filter_real = filter_ref[place, :block, :]
        filter_imag = filter_ref[place, block:, :]
        real += own_real * filter_real + own_imag * filter_imag
        imag += own_imag * filter_real - own_real * filter_imag
    total = jnp.concatenate([real, imag], axis=0).astype(low_type)
    pulled = low_dot(high_ref[...], total) + low_dot(rest_ref[...], total)
    key_out_ref[0] = (pulled * value_ref[0]).astype(low_type)
    value_out_ref[0] = (pulled * key_ref[0]).astype(low_type)


def filter_grad_kernel(count, block, table_ref, pull_table_ref, grad_ref, *refs):
    block_refs, out_ref = refs[:count], refs[count]

    @pl.when(pl.program_id(1) == 0)
    def _():
        out_ref[...] = jnp.zeros_like(out_ref)

    grad = low_dot(pull_table_ref[...], twice(grad_ref[0]))
    grad_real, grad_imag = grad[:block], grad[block:]
    for place in range(count):
        spectrum = low_dot(table_ref[...], twice(block_refs[place][0]))
        own_real, own_imag = spectrum[:block], spectrum[block:]
        out_ref[place, :block, :] += grad_real * own_real + grad_imag * own_imag
        out_ref[place, block:, :] += grad_imag * own_real - grad_real * own_imag


def full_spec(shape):
    return pl.BlockSpec(shape, lambda *place: (0,) * len(shape))


def convolve_call(body, blocks, tables, spectrum, extras, out_types):
    seqs, block, features = blocks[0].shape
    count = len(blocks)
    width = 256
    tile = pl.BlockSpec((1, block, width), lambda column, seq: (seq, 0, column))
    in_specs = [full_spec(table.shape) for table in tables]
    operands = list(tables)
    if spectrum is not None:
        in_specs.append(pl.BlockSpec((count, 2 * block, width), lambda column, seq: (0, 0, column)))
        operands.append(spectrum)
    in_specs += [tile] * (len(extras) + count)
    operands += list(extras) + list(blocks)
    if out_types is None:
        out_shape = jax.ShapeDtypeStruct((count, 2 * block, features), jnp.float32)
        out_specs = pl.BlockSpec((count, 2 * block, width), lambda column, seq: (0, 0, column))
    else:
        out_shape = [jax.ShapeDtypeStruct((seqs, block, features), kind) for kind in out_types]
        out_specs = [tile] * len(out_types)
    return pl.pallas_call(
        functools.partial(body, count, block),
        grid=(features // width, seqs),
        in_specs=in_specs,
        out_specs=out_specs,
        out_shape=out_shape,
        compiler_params=pltpu.CompilerParams(vmem_limit_bytes=48 * 2**20),
    )(*operands)


def partner_pairs(size, step):
    return [(place, place ^ step) for place in range(size)]


def swap(values, axis, step):
    return lax.ppermute(values, axis, partner_pairs(lax.axis_size(axis), step))


def gather_blocks(own, count, sign):
    size = lax.axis_size("seq")
    parity = lax.axis_index("seq") % 2
    blocks = {0: own}
    for pair in range(1, (count + 1) // 2 + 1):
        step = sign * 2 * pair
        pairs = [(a, a + step) for a in range(size) if 0 <= a + step < size]
        blocks[2 * pair] = lax.ppermute(own, "seq", pairs)
    evens = [(a, a ^ 1) for a in range(0, size, 2)]
    odds = [(a, a ^ 1) for a in range(1, size, 2)]
    near, far = (evens, odds) if sign > 0 else (odds, evens)
    for pair in range(1, (count + 1) // 2 + 1):
        blocks[2 * pair - 1] = lax.ppermute(blocks[2 * pair - 2], "seq", near) + lax.ppermute(
            blocks[2 * pair], "seq", far
        )
    return [blocks[place] for place in range(count + 1)]


def pick(values, dim, place):
    return lax.dynamic_index_in_dim(values, place, dim, keepdims=False)


def halve(values, dim, axis, bit):
    mine = (lax.axis_index(axis) >> bit) & 1
    moved = swap(pick(values, dim, 1 - mine), axis, 1 << bit)
    return pick(values, dim, mine) + moved


def seq_shares(values):
    size = lax.axis_size("seq")
    rows, width = values.shape
    bits = size.bit_length() - 1
    cells = values.reshape([2] * bits + [rows // size, width])
    cells = halve(cells, bits - 1, "seq", 0)
    middle = width // 2 // 128 * 128
    parts = []
    for part, order in (
        (cells[..., :middle], list(range(1, bits))),
        (cells[..., middle:], list(range(bits - 1, 0, -1))),
    ):
        left = sorted(order, reverse=True)
        for bit in order:
            part = halve(part, left.index(bit), "seq", bit)
            left.remove(bit)
        parts.append(part)
    return jnp.concatenate(parts, axis=-1)


def batch_total(values):
    size = lax.axis_size("batch")
    bits = size.bit_length() - 1
    rows, width = values.shape
    for bit in range(bits):
        values = halve(values.reshape(2, -1, width), 0, "batch", bit)
    for bit in reversed(range(bits)):
        mine = (lax.axis_index("batch") >> bit) & 1
        moved = swap(values, "batch", 1 << bit)
        first = jnp.where(mine == 0, values, moved)
        last = jnp.where(mine == 0, moved, values)
        values = jnp.concatenate([first, last], axis=0)
    return values


def reduce_all(values):
    return batch_total(seq_shares(values))


def norm_parts(values):
    centered = values - jnp.mean(values, axis=-1, keepdims=True)
    inverse = lax.rsqrt(jnp.mean(centered * centered, axis=-1, keepdims=True) + norm_epsilon)
    return centered * inverse, inverse


def norm_pull(grad, unit, inverse, gain):
    scaled = grad * gain
    return inverse * (
        scaled
        - jnp.mean(scaled, axis=-1, keepdims=True)
        - unit * jnp.mean(scaled * unit, axis=-1, keepdims=True)
    )


def shape_kernel(raw_kernel):
    shrunk = raw_kernel - shrink_level * jnp.tanh(raw_kernel / shrink_level)
    padded = jnp.pad(shrunk, ((1, 1), (0, 0)))
    return (padded[:-2] + padded[1:-1] + padded[2:]) / 3.0


def wide_dot(left, right):
    return jnp.dot(left, right, preferred_element_type=jnp.float32)


def token_dot(left, right):
    return lax.dot_general(left, right, (((0,), (0,)), ((), ())), preferred_element_type=jnp.float32)


def weight_dot(left, right):
    return lax.dot_general(left, right, (((1,), (1,)), ((), ())), preferred_element_type=jnp.float32)


def on_device(
    tokens,
    first_gain,
    first_shift,
    mixer_input,
    conv_kernel,
    mixer_output,
    second_gain,
    second_shift,
    widen_weight,
    narrow_weight,
    cotangent,
):
    axis_count = lax.axis_size("seq")
    seqs_here, local_len, features = tokens.shape
    row_total = seqs_here * local_len
    tap_count = conv_kernel.shape[0]
    reach = -(-tap_count // local_len)
    block_shape = tokens.shape

    forward, inverse = half_tables(local_len)
    forward_pair = jnp.asarray(stacked_pair(forward))
    inverse_high, inverse_rest = (jnp.asarray(part) for part in split_low(inverse))
    pull_pair = jnp.asarray(stacked_pair(inverse.T))
    push_high, push_rest = (jnp.asarray(part) for part in split_low(forward.T))

    flat_tokens = tokens.reshape(row_total, features).astype(jnp.float32)
    flat_cot = cotangent.reshape(row_total, features)
    unit, scale = norm_parts(flat_tokens)
    normed_low = (unit * first_gain + first_shift).astype(low_type)
    key_value = wide_dot(normed_low, mixer_input[:, features:])
    key_rows = key_value[:, :features].reshape(block_shape)
    value_rows = key_value[:, features:].reshape(block_shape)
    product = key_rows * value_rows
    product_blocks = gather_blocks(product, reach, 1)

    query_rows = wide_dot(normed_low, mixer_input[:, :features])
    raw_kernel = conv_kernel.astype(jnp.float32)
    kernel_taps = shape_kernel(raw_kernel)
    tap_blocks = jnp.pad(kernel_taps, ((0, reach * local_len - tap_count), (0, 0))).reshape(
        reach, local_len, features
    )
    table = jnp.asarray(forward.astype(np.float32))
    tap_spectra = [jnp.dot(table, tap_blocks[place], precision=highest) for place in range(reach)]
    spectra = []
    for place in range(reach + 1):
        parts = []
        if place > 0:
            parts.append(tap_spectra[place - 1])
        if place < reach:
            parts.append(turn(tap_spectra[place], local_len))
        spectra.append(sum(parts))
    spectrum = jnp.stack(spectra)

    convolved, gated_low = convolve_call(
        convolve_kernel,
        product_blocks,
        (forward_pair, inverse_high, inverse_rest),
        spectrum,
        (query_rows.reshape(block_shape),),
        (jnp.float32, low_type),
    )
    gated_low = gated_low.reshape(row_total, features)
    middle = flat_tokens + wide_dot(gated_low, mixer_output)
    unit2, scale2 = norm_parts(middle)
    second_low = (unit2 * second_gain + second_shift).astype(low_type)
    hidden = wide_dot(second_low, widen_weight)
    spread = 0.5 * (1.0 + lax.erf(hidden / math.sqrt(2.0)))
    active_low = (hidden * spread).astype(low_type)
    block_output = (middle + wide_dot(active_low, narrow_weight)).astype(low_type)
    grad_active = weight_dot(flat_cot, narrow_weight)
    slope = spread + hidden * jnp.exp(-0.5 * hidden * hidden) * (1.0 / math.sqrt(2.0 * math.pi))
    grad_hidden = (grad_active * slope).astype(low_type)
    grad_second = weight_dot(grad_hidden, widen_weight)
    grad_second_gain = jnp.sum(grad_second * unit2, axis=0)
    grad_second_shift = jnp.sum(grad_second, axis=0)
    grad_middle = flat_cot.astype(jnp.float32) + norm_pull(grad_second, unit2, scale2, second_gain)
    grad_branch = grad_middle.astype(low_type)
    grad_gated = weight_dot(grad_branch, mixer_output)
    grad_conv = (grad_gated * query_rows).reshape(block_shape)
    grad_blocks = gather_blocks(grad_conv, reach, -1)

    grad_narrow = reduce_all(token_dot(active_low, flat_cot))
    grad_widen = reduce_all(token_dot(second_low, grad_hidden))

    grad_spectrum = convolve_call(
        filter_grad_kernel, product_blocks, (forward_pair, pull_pair), None, (grad_conv,), None
    )
    back_table = jnp.asarray(forward.T.astype(np.float32))
    grad_taps = jnp.concatenate(
        [
            jnp.dot(
                back_table,
                grad_spectrum[place + 1] + turn_back(grad_spectrum[place], local_len),
                precision=highest,
            )
            for place in range(reach)
        ]
    )[:tap_count]
    padded = jnp.pad(grad_taps, ((1, 1), (0, 0)))
    grad_kernel = (
        (padded[:-2] + padded[1:-1] + padded[2:]) / 3.0 * jnp.tanh(raw_kernel / shrink_level) ** 2
    )
    lanes = 128
    kernel_width = tap_count * features // features
    second_sums = jnp.stack([grad_second_gain, grad_second_shift], axis=1)
    mixed_group = jnp.concatenate(
        [
            token_dot(gated_low, grad_branch),
            grad_kernel.reshape(features, kernel_width),
            jnp.pad(second_sums, ((0, 0), (0, lanes - 2))),
        ],
        axis=1,
    )
    output_sum = reduce_all(mixed_group)

    grad_key, grad_value = convolve_call(
        pull_kernel,
        grad_blocks,
        (pull_pair, push_high, push_rest),
        spectrum,
        (key_rows, value_rows),
        (low_type, low_type),
    )
    grad_query = (grad_gated * convolved.reshape(row_total, features)).astype(low_type)
    grad_mixed = jnp.concatenate(
        [
            grad_query,
            grad_key.reshape(row_total, features),
            grad_value.reshape(row_total, features),
        ],
        axis=1,
    )
    grad_normed = weight_dot(grad_mixed, mixer_input)
    first_sums = jnp.stack([jnp.sum(grad_normed * unit, axis=0), jnp.sum(grad_normed, axis=0)], axis=1)
    input_group = jnp.concatenate(
        [token_dot(normed_low, grad_mixed), jnp.pad(first_sums, ((0, 0), (0, lanes - 2)))], axis=1
    )
    input_sum = reduce_all(input_group)
    grad_tokens = (grad_middle + norm_pull(grad_normed, unit, scale, first_gain)).astype(low_type)

    side = 3 * features
    edge = features + kernel_width
    return (
        block_output.reshape(block_shape),
        grad_tokens.reshape(block_shape),
        input_sum[:, side],
        input_sum[:, side + 1],
        input_sum[:, :side],
        output_sum[:, features:edge].reshape(tap_count // axis_count, features),
        output_sum[:, :features],
        output_sum[:, edge],
        output_sum[:, edge + 1],
        grad_widen,
        grad_narrow,
    )


def solution(mesh):
    in_specs = (
        P("batch", "seq", None),
        P(),
        P(),
        P(),
        P(),
        P(),
        P(),
        P(),
        P(),
        P(),
        P("batch", "seq", None),
    )
    out_specs = (
        P("batch", "seq", None),
        P("batch", "seq", None),
        P("seq"),
        P("seq"),
        P("seq", None),
        P("seq", None),
        P("seq", None),
        P("seq"),
        P("seq"),
        P("seq", None),
        P("seq", None),
    )
    return jax.shard_map(
        on_device, mesh=mesh, in_specs=in_specs, out_specs=out_specs, check_vma=False
    )
```

time: 1040 us -> 468 us (0.45)
  blocking collectives: 265 us -> 0 us
  waiting for transfers between devices: 406 us -> 233 us
  matrix products: 172 us -> 52.7 us
  local copies, waits for them, and re-layouts: 129 us -> 29.7 us
  starting transfers between devices: 15.8 us -> 64.8 us
  Pallas kernels: 0 us -> 32.4 us
  other arithmetic: 27.5 us -> 47.7 us
  between operations: 15.8 us -> 2.58 us
    all_to_all x5 -> x0, blocking collectives: 253 us -> none  [the longest x2 176 us: spread_inverse(): lax.all_to_all(turned, 'seq', split_axis=3, concat_axis=2, tiled=True)]
    ppermute x0 -> x42, waiting for transfers between devices: none -> 233 us  [the longest x36 203 us: swap(): return lax.ppermute(values, axis, partner_pairs(lax.axis_size(axis), step))]
    all_to_all x3 -> x0, waiting for transfers between devices: 154 us -> none  [the longest x2 133 us: spread_forward(): lax.all_to_all(turned, 'seq', split_axis=2, concat_axis=3, tiled=True)]
    psum x1 -> x0, waiting for transfers between devices: 128 us -> none  [on_device(): lax.psum((row_input, row_kernel, row_output, row_widen, row_narrow, row_n...]
    dot_general x40 -> x17, matrix products: 172 us -> 52.7 us  [the longest x5 20.1 us: wide_dot(): return jnp.dot(left, right, preferred_element_type=jnp.float32)]
    reduce_scatter x5 -> x0, waiting for transfers between devices: 96.4 us -> none  [the longest x1 69.3 us: on_device(): lax.psum_scatter(grad_mixer_input, 'seq', scatter_dimension=0, tiled=True)]
    ppermute x0 -> x42, starting transfers between devices: none -> 64.8 us  [the longest x36 49.5 us: swap(): return lax.ppermute(values, axis, partner_pairs(lax.axis_size(axis), step))]
    another operation x11 -> x5, local copies, waits for them, and re-layouts: 40 us -> 0.2 us  [the longest x3 0.19 us: on_device(): jnp.stack([jnp.sum(grad_normed * unit, axis=0), jnp.sum(grad_normed, axis...]
  transfers between devices with their start and end apart: 10 -> 42, of which waited for: 7 -> 20; matrix products, arithmetic and copies ran while one was open for 16% -> 15% of each run, Pallas kernels for 0% -> 2%
where the time goes in v1:
time: 468 us; the launch traced here: 463 us
  waiting for transfers between devices  233 us (50%)
  starting transfers between devices  64.8 us (14%)
  matrix products  52.7 us (11%)
  other arithmetic  47.7 us (10%)
  Pallas kernels  32.4 us (7%)
  local copies, waits for them, and re-layouts  29.7 us (6%)
    ppermute x36, waiting for transfers between devices, swap(): return lax.ppermute(values, axis, partner_pairs(lax.axis_size(axis), step))  203 us
    ppermute x36, starting transfers between devices, swap(): return lax.ppermute(values, axis, partner_pairs(lax.axis_size(axis), step))  49.5 us
    pallas_call x3, Pallas kernels, convolve_call(): pl.pallas_call(functools.partial(body, count, block), grid=(features // w...  32.4 us
    ppermute x2, waiting for transfers between devices, gather_blocks(): blocks[2 * pair] = lax.ppermute(own, 'seq', pairs)  29.9 us
    dot_general x5, matrix products, wide_dot(): return jnp.dot(left, right, preferred_element_type=jnp.float32)  20.1 us
    dot_general x4, matrix products, token_dot(): lax.dot_general(left, right, (((0,), (0,)), ((), ())), preferred_element_...  14.5 us
    dot_general x4, matrix products, weight_dot(): lax.dot_general(left, right, (((1,), (1,)), ((), ())), preferred_element_...  14.4 us
    add x28, other arithmetic, halve(): return pick(values, dim, mine) + moved  14 us
  transfers between devices with their start and end apart: 42, of which 20 were waited for; matrix products, arithmetic and copies ran while one was open for 15% of the time, Pallas kernels for 2%

profile of v1, /device:TPU:0, one launch (start us, length us, event | category | flops | bytes accessed | tf_op | source)
XLA Modules:
  0.0 462.7 jit_solution(15237649611292604217)
XLA Ops:
  5.6 3.0 fusion.11
  10.6 6.1 %collective-permute-start.1 = (f32[4,128,768]{2,1,0:T(8,128)}, f32[4,128,768]{2,1,0:T(8,128)}, u32[]{:S(2)}, u32[]{:S(2)}) collective-permute-start(f32[4,128,768]{2,1,0:T(8,128)} %mul.150.refs_0_), channel_id=1, source_target_pairs={{0,8},{4,12},{8,16},{12,20},{16,24},{20,28},{1,9},{5,13},{9,17},{1... | collective-permute-start | bytes 4718600 | tf_op jit(solution)/shard_map/ppermute | solution.py:157
  16.7 2.6 collective-permute-start
  19.7 29.9 %collective-permute-done.1.refs_2_ = f32[4,128,768]{2,1,0:T(8,128)} collective-permute-done((f32[4,128,768]{2,1,0:T(8,128)}, f32[4,128,768]{2,1,0:T(8,128)}, u32[]{:S(2)}, u32[]{:S(2)}) %collective-permute-start.1) | collective-permute-done | bytes 1572896 | tf_op jit(solution)/shard_map/ppermute | solution.py:157
  58.4 3.9 add.291.refs_1_
  62.4 11.0 %shard_map.266 = (f32[4,128,768]{2,1,0:T(8,128)S(1)}, bf16[4,128,768]{2,1,0:T(8,128)(2,1)S(1)}) custom-call(bf16[256,256]{1,0:T(8,128)(2,1)S(1)} %copy-done.10, bf16[128,256]{1,0:T(8,128)(2,1)S(1)} %copy-done.15, bf16[128,256]{1,0:T(8,128)(2,1)S(1)} %copy-done.14, f32[3,256,768]{2,1,0:T(8,128)} %pad_maximum_fusion.1.filter_ref, ...), custom_call_target="tpu_custom_call" | custom-call | tf_op jit(solution)/shard_map/pallas_call | solution.py:132
  78.2 7.0 %fusion.9 = (bf16[3072,512]{0,1:T(8,128)(2,1)}, f32[512,3072]{1,0:T(8,128)S(1)}) fusion(bf16[768,3072]{1,0:T(8,128)(2,1)} %param.27, f32[512,768]{1,0:T(8,128)S(1)} %get-tuple-element.74, f32[768]{0:T(1024)S(1)} %copy-done.49, f32[768]{0:T(1024)S(1)} %copy-done.46, f32[512]{0:T(512)S(1)} %add_rsqrt_fusion, f32[512]{0:T(512)S(1)} %broadcast_multiply_fusion.4), kind=kOutput, calls=%fused_computation.16 | convolution fusion | flops 2425749504 | bytes 15738880 | tf_op jit(solution)/shard_map/dot_general | solution.py:239
  85.3 4.3 fusion.5
  89.7 4.1 multiply_reduce_fusion
  95.9 2.6 multiply_add_fusion
  103.4 10.3 %shard_map.268 = f32[3,256,768]{2,1,0:T(8,128)} custom-call(bf16[256,256]{1,0:T(8,128)(2,1)S(1)} %copy-done.11, bf16[256,256]{1,0:T(8,128)(2,1)S(1)} %copy-done.9, f32[4,128,768]{2,1,0:T(8,128)} %bitcast.13.refs_0_.grad_ref, f32[4,128,768]{2,1,0:T(8,128)} %mul.150.refs_0_, f32[4,128,768]{2,1,0:T(8,128)S(1)} %copy-done.4, ...), custom_call_target="tpu_custom_call" | custom-call | tf_op jit(solution)/shard_map/pallas_call | solution.py:132
  125.7 3.7 collective-permute-done.15
  131.8 2.6 collective-permute-start.16
  136.0 6.0 %add_convert_fusion = bf16[512,768]{1,0:T(8,128)(2,1)} fusion(f32[512,768]{1,0:T(8,128)S(1)} %copy-done.26, bf16[3072,768]{1,0:T(8,128)(2,1)S(1)} %bitcast.296, f32[512,3072]{1,0:T(8,128)} %copy-done.53), kind=kOutput, calls=%fused_computation.55 | convolution fusion | flops 2424569856 | bytes 13369344 | tf_op jit(solution)/shard_map/dot_general | solution.py:239
  145.0 3.6 collective-permute-start.17
  149.5 2.9 fusion.80
  152.6 33.1 %collective-permute-done.19 = f32[96,640]{1,0:T(8,128)S(1)} collective-permute-done((f32[96,640]{1,0:T(8,128)S(1)}, f32[96,640]{1,0:T(8,128)S(1)}, u32[]{:S(2)}, u32[]{:S(2)}) %collective-permute-start.19) | collective-permute-done | bytes 245792 | tf_op jit(solution)/shard_map/ppermute | solution.py:147
  187.5 2.7 dynamic-slice_bitcast_fusion.1
  190.2 4.7 %copy.43 = bf16[3072,512]{1,0:T(8,128)(2,1)} copy(bf16[3072,512]{0,1:T(8,128)(2,1)} %get-tuple-element.78) | data formatting | bytes 6291456 | tf_op jit(solution)/shard_map/dot_general | solution.py:243
  197.5 2.7 collective-permute-start.21
  200.2 4.5 fusion.88
  205.9 2.9 dynamic-slice_bitcast_fusion
  212.1 2.8 add.301.refs_1_
  215.0 11.1 %shard_map.267 = (bf16[4,128,768]{2,1,0:T(8,128)(2,1)S(1)}, bf16[4,128,768]{2,1,0:T(8,128)(2,1)S(1)}) custom-call(bf16[256,256]{1,0:T(8,128)(2,1)S(1)} %copy-done.9, bf16[128,256]{1,0:T(8,128)(2,1)S(1)} %copy-done.13, bf16[128,256]{1,0:T(8,128)(2,1)S(1)} %copy-done.12, f32[3,256,768]{2,1,0:T(8,128)} %pad_maximum_fusion.1.filter_ref, ...), custom_call_target="tpu_custom_call" | custom-call | tf_op jit(solution)/shard_map/pallas_call | solution.py:132
  226.1 3.7 fusion.28
  229.9 4.9 %fusion.31 = f32[768,2304]{1,0:T(8,128)} fusion(bf16[512,768]{1,0:T(8,128)(2,1)S(1)} %copy-done.37, bf16[512,768]{1,0:T(8,128)(2,1)S(1)} %bitcast.259, bf16[512,768]{1,0:T(8,128)(2,1)S(1)} %bitcast.257, bf16[512,768]{1,0:T(8,128)(2,1)S(1)} %copy-done.38), kind=kOutput, calls=%fused_computation.79 | convolution fusion | flops 1819017216 | bytes 10223616 | tf_op jit(solution)/shard_map/dot_general | solution.py:243
  235.0 3.5 select_maximum_fusion
  240.7 2.6 copy-done.16
  246.9 4.7 %bitcast_add_fusion.1 = f32[2,2,96,3072]{3,2,1,0:T(8,128)S(1)} fusion(f32[2,2,96,3072]{3,2,1,0:T(8,128)} %collective-permute-done.24, f32[2,2,2,96,3072]{4,3,2,1,0:T(8,128)} %bitcast.265, s32[]{:T(128)S(6)} %select_n.200), kind=kLoop, calls=%fused_computation.18 | loop fusion | flops 1179648 | bytes 14155780 | tf_op jit(solution)/shard_map/add | solution.py:175
  255.3 3.0 bitcast_add_fusion
  260.1 20.9 %collective-permute-done.27 = f32[2,96,1536]{2,1,0:T(8,128)S(1)} collective-permute-done((f32[2,96,1536]{2,1,0:T(8,128)S(1)}, f32[2,96,1536]{2,1,0:T(8,128)S(1)}, u32[]{:S(2)}, u32[]{:S(2)}) %collective-permute-start.27) | collective-permute-done | bytes 1179680 | tf_op jit(solution)/shard_map/ppermute | solution.py:147
  284.5 21.8 %collective-permute-done.36 = f32[2,384,384]{2,1,0:T(8,128)S(1)} collective-permute-done((f32[2,384,384]{2,1,0:T(8,128)S(1)}, f32[2,384,384]{2,1,0:T(8,128)S(1)}, u32[]{:S(2)}, u32[]{:S(2)}) %collective-permute-start.36) | collective-permute-done | bytes 1179680 | tf_op jit(solution)/shard_map/ppermute | solution.py:147
  309.7 10.4 %collective-permute-done.28 = f32[96,1536]{1,0:T(8,128)S(1)} collective-permute-done((f32[96,1536]{1,0:T(8,128)S(1)}, f32[96,1536]{1,0:T(8,128)S(1)}, u32[]{:S(2)}, u32[]{:S(2)}) %collective-permute-start.28) | collective-permute-done | bytes 589856 | tf_op jit(solution)/shard_map/ppermute | solution.py:147
  322.4 9.8 %collective-permute-done.37 = f32[384,384]{1,0:T(8,128)S(1)} collective-permute-done((f32[384,384]{1,0:T(8,128)S(1)}, f32[384,384]{1,0:T(8,128)S(1)}, u32[]{:S(2)}, u32[]{:S(2)}) %collective-permute-start.37) | collective-permute-done | bytes 589856 | tf_op jit(solution)/shard_map/ppermute | solution.py:147
  334.5 2.5 bitcast_add_fusion.2
  340.2 13.7 %collective-permute-done.38 = f32[192,768]{1,0:T(8,128)S(1)} collective-permute-done((f32[192,768]{1,0:T(8,128)S(1)}, f32[192,768]{1,0:T(8,128)S(1)}, u32[]{:S(2)}, u32[]{:S(2)}) %collective-permute-start.38) | collective-permute-done | bytes 589856 | tf_op jit(solution)/shard_map/ppermute | solution.py:147
  354.1 3.0 collective-permute-start.31
  357.1 17.5 %collective-permute-done.39 = f32[96,768]{1,0:T(8,128)S(1)} collective-permute-done((f32[96,768]{1,0:T(8,128)S(1)}, f32[96,768]{1,0:T(8,128)S(1)}, u32[]{:S(2)}, u32[]{:S(2)}) %collective-permute-start.39) | collective-permute-done | bytes 294944 | tf_op jit(solution)/shard_map/ppermute | solution.py:147
  374.8 7.1 %collective-permute-start.8 = (f32[96,1152]{1,0:T(8,128)S(1)}, f32[96,1152]{1,0:T(8,128)S(1)}, u32[]{:S(2)}, u32[]{:S(2)}) collective-permute-start(f32[96,1152]{1,0:T(8,128)S(1)} %dynamic-slice_bitcast_fusion.19), channel_id=1, source_target_pairs={{0,16},{4,20},{8,24},{12,28},{16,0},{20,4},{24,8},{28,12},{1,17},{... | collective-permute-start | bytes 1327112 | tf_op jit(solution)/shard_map/ppermute | solution.py:147
  382.2 5.0 %collective-permute-done.31 = f32[24,3072]{1,0:T(8,128)S(1)} collective-permute-done((f32[24,3072]{1,0:T(8,128)S(1)}, f32[24,3072]{1,0:T(8,128)S(1)}, u32[]{:S(2)}, u32[]{:S(2)}) %collective-permute-start.31) | collective-permute-done | bytes 294944 | tf_op jit(solution)/shard_map/ppermute | solution.py:147
  387.3 5.0 %collective-permute-done.8 = f32[96,1152]{1,0:T(8,128)S(1)} collective-permute-done((f32[96,1152]{1,0:T(8,128)S(1)}, f32[96,1152]{1,0:T(8,128)S(1)}, u32[]{:S(2)}, u32[]{:S(2)}) %collective-permute-start.8) | collective-permute-done | bytes 442400 | tf_op jit(solution)/shard_map/ppermute | solution.py:147
  392.3 2.7 collective-permute-done.10
  397.5 13.8 %collective-permute-done.11 = f32[48,2432]{1,0:T(8,128)S(1)} collective-permute-done((f32[48,2432]{1,0:T(8,128)S(1)}, f32[48,2432]{1,0:T(8,128)S(1)}, u32[]{:S(2)}, u32[]{:S(2)}) %collective-permute-start.11) | collective-permute-done | bytes 466976 | tf_op jit(solution)/shard_map/ppermute | solution.py:147
  411.6 14.9 %collective-permute-done.32 = f32[48,3072]{1,0:T(8,128)S(1)} collective-permute-done((f32[48,3072]{1,0:T(8,128)S(1)}, f32[48,3072]{1,0:T(8,128)S(1)}, u32[]{:S(2)}, u32[]{:S(2)}) %collective-permute-start.32) | collective-permute-done | bytes 589856 | tf_op jit(solution)/shard_map/ppermute | solution.py:147
  426.6 8.0 %collective-permute-done.12 = f32[24,2432]{1,0:T(8,128)S(1)} collective-permute-done((f32[24,2432]{1,0:T(8,128)S(1)}, f32[24,2432]{1,0:T(8,128)S(1)}, u32[]{:S(2)}, u32[]{:S(2)}) %collective-permute-start.12) | collective-permute-done | bytes 233504 | tf_op jit(solution)/shard_map/ppermute | solution.py:147
  434.7 3.4 collective-permute-start.13
  438.2 10.4 %collective-permute-done.13 = f32[24,2432]{1,0:T(8,128)S(1)} collective-permute-done((f32[24,2432]{1,0:T(8,128)S(1)}, f32[24,2432]{1,0:T(8,128)S(1)}, u32[]{:S(2)}, u32[]{:S(2)}) %collective-permute-start.13) | collective-permute-done | bytes 233504 | tf_op jit(solution)/shard_map/ppermute | solution.py:147
  450.9 9.5 %collective-permute-done.14 = f32[48,2432]{1,0:T(8,128)S(1)} collective-permute-done((f32[48,2432]{1,0:T(8,128)S(1)}, f32[48,2432]{1,0:T(8,128)S(1)}, u32[]{:S(2)}, u32[]{:S(2)}) %collective-permute-start.14) | collective-permute-done | bytes 466976 | tf_op jit(solution)/shard_map/ppermute | solution.py:147
  (318 shorter events, 90.2 us)
Async XLA Ops:
  0.6 75.1 %copy-start = (bf16[768,768]{1,0:T(8,128)(2,1)S(1)}, bf16[768,768]{1,0:T(8,128)(2,1)}, u32[]{:S(2)}) copy-start(bf16[768,768]{1,0:T(8,128)(2,1)} %param.24) | copy-start | bytes 3538948
  10.6 40.2 %copy-start.40 = (f32[256,128]{1,0:T(8,128)S(1)}, f32[256,128]{1,0:T(8,128)}, u32[]{:S(2)}) copy-start(f32[256,128]{1,0:T(8,128)} %constant.241.clone) | copy-start | bytes 393220
  10.6 38.9 %collective-permute-start.1 = (f32[4,128,768]{2,1,0:T(8,128)}, f32[4,128,768]{2,1,0:T(8,128)}, u32[]{:S(2)}, u32[]{:S(2)}) collective-permute-start(f32[4,128,768]{2,1,0:T(8,128)} %mul.150.refs_0_), channel_id=1, source_target_pairs={{0,8},{4,12},{8,16},{12,20},{16,24},{20,28},{1,9},{5,13},{9,17},{1... | collective-permute-start | bytes 4718600 | tf_op jit(solution)/shard_map/ppermute | solution.py:157
  16.7 41.7 %collective-permute-start = (f32[4,128,768]{2,1,0:T(8,128)}, f32[4,128,768]{2,1,0:T(8,128)}, u32[]{:S(2)}, u32[]{:S(2)}) collective-permute-start(f32[4,128,768]{2,1,0:T(8,128)} %mul.150.refs_0_), channel_id=1, source_target_pairs={{0,4},{8,12},{16,20},{24,28},{1,5},{9,13},{17,21},{25,29},{2,6},{1... | collective-permute-start | bytes 4718600 | tf_op jit(solution)/shard_map/ppermute | solution.py:162
  19.7 31.2 %copy-start.28 = (f32[256,768]{1,0:T(8,128)}, f32[256,768]{1,0:T(8,128)S(1)}, u32[]{:S(2)}) copy-start(f32[256,768]{1,0:T(8,128)S(1)} %add_multiply_fusion.1) | copy-start | bytes 2359300
  49.5 8.9 %collective-permute-start.2 = (f32[4,128,768]{2,1,0:T(8,128)}, f32[4,128,768]{2,1,0:T(8,128)}, u32[]{:S(2)}, u32[]{:S(2)}) collective-permute-start(f32[4,128,768]{2,1,0:T(8,128)} %collective-permute-done.1.refs_2_), channel_id=1, source_target_pairs={{4,0},{12,8},{20,16},{28,24},{5,1},{13,9},{21,17},{29,25},{6,2},{1... | collective-permute-start | bytes 4718600 | tf_op jit(solution)/shard_map/ppermute | solution.py:162
  121.0 15.0 %slice-start.9 = ((s8[4718592]{0:T(1024)(128)(4,1)}), s8[524288]{0:T(1024)(128)(4,1)S(1)}, s32[]{:S(2)}) async-start(s8[4718592]{0:T(1024)(128)(4,1)} %bitcast.295), calls=%async_computation.9 | async-start | bytes 1048576
  123.5 5.9 %collective-permute-start.15 = (f32[2,2,96,1152]{3,2,1,0:T(8,128)}, f32[2,2,96,1152]{3,2,1,0:T(8,128)}, u32[]{:S(2)}, u32[]{:S(2)}) collective-permute-start(f32[2,2,96,1152]{3,2,1,0:T(8,128)} %dynamic-slice_bitcast_fusion.3), channel_id=1, source_target_pairs={{0,4},{4,0},{8,12},{12,8},{16,20},{20,16},{24,28},{28,24},{1,5},{5... | collective-permute-start | bytes 5308424 | tf_op jit(solution)/shard_map/ppermute | solution.py:147
  131.8 13.1 %collective-permute-start.16 = (f32[2,96,512]{2,1,0:T(8,128)S(1)}, f32[2,96,512]{2,1,0:T(8,128)S(1)}, u32[]{:S(2)}, u32[]{:S(2)}) collective-permute-start(f32[2,96,512]{2,1,0:T(8,128)S(1)} %dynamic-slice_bitcast_fusion.20), channel_id=1, source_target_pairs={{0,8},{4,12},{8,0},{12,4},{16,24},{20,28},{24,16},{28,20},{1,9},{5... | collective-permute-start | bytes 1179656 | tf_op jit(solution)/shard_map/ppermute | solution.py:147
  134.4 14.2 %collective-permute-start.18 = (f32[2,96,640]{2,1,0:T(8,128)S(1)}, f32[2,96,640]{2,1,0:T(8,128)S(1)}, u32[]{:S(2)}, u32[]{:S(2)}) collective-permute-start(f32[2,96,640]{2,1,0:T(8,128)S(1)} %dynamic-slice_bitcast_fusion.16), channel_id=1, source_target_pairs={{0,16},{4,20},{8,24},{12,28},{16,0},{20,4},{24,8},{28,12},{1,17},{... | collective-permute-start | bytes 1474568 | tf_op jit(solution)/shard_map/ppermute | solution.py:147
  142.0 53.0 %collective-permute-start.4 = (f32[4,128,768]{2,1,0:T(8,128)}, f32[4,128,768]{2,1,0:T(8,128)}, u32[]{:S(2)}, u32[]{:S(2)}) collective-permute-start(f32[4,128,768]{2,1,0:T(8,128)} %bitcast.13.refs_0_.grad_ref), channel_id=1, source_target_pairs={{8,0},{12,4},{16,8},{20,12},{24,16},{28,20},{9,1},{13,5},{17,9},{2... | collective-permute-start | bytes 4718600 | tf_op jit(solution)/shard_map/ppermute | solution.py:157
  143.6 68.5 %collective-permute-start.3 = (f32[4,128,768]{2,1,0:T(8,128)}, f32[4,128,768]{2,1,0:T(8,128)}, u32[]{:S(2)}, u32[]{:S(2)}) collective-permute-start(f32[4,128,768]{2,1,0:T(8,128)} %bitcast.13.refs_0_.grad_ref), channel_id=1, source_target_pairs={{4,0},{12,8},{20,16},{28,24},{5,1},{13,9},{21,17},{29,25},{6,2},{1... | collective-permute-start | bytes 4718600 | tf_op jit(solution)/shard_map/ppermute | solution.py:162
  145.0 7.6 %collective-permute-start.17 = (f32[96,512]{1,0:T(8,128)S(1)}, f32[96,512]{1,0:T(8,128)S(1)}, u32[]{:S(2)}, u32[]{:S(2)}) collective-permute-start(f32[96,512]{1,0:T(8,128)S(1)} %dynamic-slice_bitcast_fusion.26), channel_id=1, source_target_pairs={{0,16},{4,20},{8,24},{12,28},{16,0},{20,4},{24,8},{28,12},{1,17},{... | collective-permute-start | bytes 589832 | tf_op jit(solution)/shard_map/ppermute | solution.py:147
  148.6 37.1 %collective-permute-start.19 = (f32[96,640]{1,0:T(8,128)S(1)}, f32[96,640]{1,0:T(8,128)S(1)}, u32[]{:S(2)}, u32[]{:S(2)}) collective-permute-start(f32[96,640]{1,0:T(8,128)S(1)} %dynamic-slice_bitcast_fusion.23), channel_id=1, source_target_pairs={{0,8},{4,12},{8,0},{12,4},{16,24},{20,28},{24,16},{28,20},{1,9},{5... | collective-permute-start | bytes 737288 | tf_op jit(solution)/shard_map/ppermute | solution.py:147
  152.4 37.8 %copy-start.23 = (f32[768,3072]{1,0:T(8,128)}, f32[768,3072]{1,0:T(8,128)S(1)}, u32[]{:S(2)}) copy-start(f32[768,3072]{1,0:T(8,128)S(1)} %fusion.80) | copy-start | bytes 28311556
  185.8 11.6 %collective-permute-start.20 = (f32[48,1152]{1,0:T(8,128)S(1)}, f32[48,1152]{1,0:T(8,128)S(1)}, u32[]{:S(2)}, u32[]{:S(2)}) collective-permute-start(f32[48,1152]{1,0:T(8,128)S(1)} %dynamic-slice_bitcast_fusion.25), channel_id=1, source_target_pairs={{0,1},{1,0},{2,3},{3,2},{4,5},{5,4},{6,7},{7,6},{8,9},{9,8},{10,11... | collective-permute-start | bytes 663560 | tf_op jit(solution)/shard_map/ppermute | solution.py:147
  194.9 52.0 %collective-permute-start.24 = (f32[2,2,96,3072]{3,2,1,0:T(8,128)}, f32[2,2,96,3072]{3,2,1,0:T(8,128)}, u32[]{:S(2)}, u32[]{:S(2)}) collective-permute-start(f32[2,2,96,3072]{3,2,1,0:T(8,128)} %dynamic-slice_bitcast_fusion.1), channel_id=1, source_target_pairs={{0,4},{4,0},{8,12},{12,8},{16,20},{20,16},{24,28},{28,24},{1,5},{5... | collective-permute-start | bytes 14155784 | tf_op jit(solution)/shard_map/ppermute | solution.py:147
  194.9 17.2 %collective-permute-start.5 = (f32[4,128,768]{2,1,0:T(8,128)}, f32[4,128,768]{2,1,0:T(8,128)S(1)}, u32[]{:S(2)}, u32[]{:S(2)}) collective-permute-start(f32[4,128,768]{2,1,0:T(8,128)} %collective-permute-done.4.refs_2_), channel_id=1, source_target_pairs={{0,4},{8,12},{16,20},{24,28},{1,5},{9,13},{17,21},{25,29},{2,6},{1... | collective-permute-start | bytes 4718600 | tf_op jit(solution)/shard_map/ppermute | solution.py:162
  197.5 7.5 %collective-permute-start.21 = (f32[24,1152]{1,0:T(8,128)S(1)}, f32[24,1152]{1,0:T(8,128)S(1)}, u32[]{:S(2)}, u32[]{:S(2)}) collective-permute-start(f32[24,1152]{1,0:T(8,128)S(1)} %dynamic-slice_bitcast_fusion.27), channel_id=1, source_target_pairs={{0,2},{1,3},{2,0},{3,1},{4,6},{5,7},{6,4},{7,5},{8,10},{9,11},{10,... | collective-permute-start | bytes 331784 | tf_op jit(solution)/shard_map/ppermute | solution.py:147
  205.0 6.9 %collective-permute-start.22 = (f32[24,1152]{1,0:T(8,128)S(1)}, f32[24,1152]{1,0:T(8,128)S(1)}, u32[]{:S(2)}, u32[]{:S(2)}) collective-permute-start(f32[24,1152]{1,0:T(8,128)S(1)} %bitcast_add_fusion.28), channel_id=1, source_target_pairs={{0,2},{1,3},{2,0},{3,1},{4,6},{5,7},{6,4},{7,5},{8,10},{9,11},{10,... | collective-permute-start | bytes 331784 | tf_op jit(solution)/shard_map/ppermute | solution.py:147
  209.7 45.7 %collective-permute-start.33 = (f32[2,2,384,768]{3,2,1,0:T(8,128)}, f32[2,2,384,768]{3,2,1,0:T(8,128)}, u32[]{:S(2)}, u32[]{:S(2)}) collective-permute-start(f32[2,2,384,768]{3,2,1,0:T(8,128)} %dynamic-slice_bitcast_fusion), channel_id=1, source_target_pairs={{0,4},{4,0},{8,12},{12,8},{16,20},{20,16},{24,28},{28,24},{1,5},{5... | collective-permute-start | bytes 14155784 | tf_op jit(solution)/shard_map/ppermute | solution.py:147
  212.0 32.8 %collective-permute-start.23 = (f32[48,1152]{1,0:T(8,128)S(1)}, f32[48,1152]{1,0:T(8,128)S(1)}, u32[]{:S(2)}, u32[]{:S(2)}) collective-permute-start(f32[48,1152]{1,0:T(8,128)S(1)} %pad_maximum_fusion.16), channel_id=1, source_target_pairs={{0,1},{1,0},{2,3},{3,2},{4,5},{5,4},{6,7},{7,6},{8,9},{9,8},{10,11... | collective-permute-start | bytes 663560 | tf_op jit(solution)/shard_map/ppermute | solution.py:147
  243.3 91.2 %collective-permute-start.6 = (f32[2,2,96,2432]{3,2,1,0:T(8,128)}, f32[2,2,96,2432]{3,2,1,0:T(8,128)}, u32[]{:S(2)}, u32[]{:S(2)}) collective-permute-start(f32[2,2,96,2432]{3,2,1,0:T(8,128)} %dynamic-slice_bitcast_fusion.2), channel_id=1, source_target_pairs={{0,4},{4,0},{8,12},{12,8},{16,20},{20,16},{24,28},{28,24},{1,5},{5... | collective-permute-start | bytes 11206664 | tf_op jit(solution)/shard_map/ppermute | solution.py:147
  252.1 28.8 %collective-permute-start.27 = (f32[2,96,1536]{2,1,0:T(8,128)S(1)}, f32[2,96,1536]{2,1,0:T(8,128)S(1)}, u32[]{:S(2)}, u32[]{:S(2)}) collective-permute-start(f32[2,96,1536]{2,1,0:T(8,128)S(1)} %dynamic-slice_bitcast_fusion.6), channel_id=1, source_target_pairs={{0,16},{4,20},{8,24},{12,28},{16,0},{20,4},{24,8},{28,12},{1,17},{... | collective-permute-start | bytes 3538952 | tf_op jit(solution)/shard_map/ppermute | solution.py:147
  253.4 29.1 %collective-permute-start.25 = (f32[2,96,1536]{2,1,0:T(8,128)S(1)}, f32[2,96,1536]{2,1,0:T(8,128)S(1)}, u32[]{:S(2)}, u32[]{:S(2)}) collective-permute-start(f32[2,96,1536]{2,1,0:T(8,128)S(1)} %dynamic-slice_bitcast_fusion.7), channel_id=1, source_target_pairs={{0,8},{4,12},{8,0},{12,4},{16,24},{20,28},{24,16},{28,20},{1,9},{5... | collective-permute-start | bytes 3538952 | tf_op jit(solution)/shard_map/ppermute | solution.py:147
  258.7 47.5 %collective-permute-start.36 = (f32[2,384,384]{2,1,0:T(8,128)S(1)}, f32[2,384,384]{2,1,0:T(8,128)S(1)}, u32[]{:S(2)}, u32[]{:S(2)}) collective-permute-start(f32[2,384,384]{2,1,0:T(8,128)S(1)} %dynamic-slice_bitcast_fusion.4), channel_id=1, source_target_pairs={{0,16},{4,20},{8,24},{12,28},{16,0},{20,4},{24,8},{28,12},{1,17},{... | collective-permute-start | bytes 3538952 | tf_op jit(solution)/shard_map/ppermute | solution.py:147
  259.2 48.6 %collective-permute-start.34 = (f32[2,384,384]{2,1,0:T(8,128)S(1)}, f32[2,384,384]{2,1,0:T(8,128)S(1)}, u32[]{:S(2)}, u32[]{:S(2)}) collective-permute-start(f32[2,384,384]{2,1,0:T(8,128)S(1)} %dynamic-slice_bitcast_fusion.5), channel_id=1, source_target_pairs={{0,8},{4,12},{8,0},{12,4},{16,24},{20,28},{24,16},{28,20},{1,9},{5... | collective-permute-start | bytes 3538952 | tf_op jit(solution)/shard_map/ppermute | solution.py:147
  281.2 39.0 %collective-permute-start.28 = (f32[96,1536]{1,0:T(8,128)S(1)}, f32[96,1536]{1,0:T(8,128)S(1)}, u32[]{:S(2)}, u32[]{:S(2)}) collective-permute-start(f32[96,1536]{1,0:T(8,128)S(1)} %dynamic-slice_bitcast_fusion.14), channel_id=1, source_target_pairs={{0,8},{4,12},{8,0},{12,4},{16,24},{20,28},{24,16},{28,20},{1,9},{5... | collective-permute-start | bytes 1769480 | tf_op jit(solution)/shard_map/ppermute | solution.py:147
  282.7 37.5 %collective-permute-start.26 = (f32[96,1536]{1,0:T(8,128)S(1)}, f32[96,1536]{1,0:T(8,128)S(1)}, u32[]{:S(2)}, u32[]{:S(2)}) collective-permute-start(f32[96,1536]{1,0:T(8,128)S(1)} %dynamic-slice_bitcast_fusion.15), channel_id=1, source_target_pairs={{0,16},{4,20},{8,24},{12,28},{16,0},{20,4},{24,8},{28,12},{1,17},{... | collective-permute-start | bytes 1769480 | tf_op jit(solution)/shard_map/ppermute | solution.py:147
  306.4 25.8 %collective-permute-start.37 = (f32[384,384]{1,0:T(8,128)S(1)}, f32[384,384]{1,0:T(8,128)S(1)}, u32[]{:S(2)}, u32[]{:S(2)}) collective-permute-start(f32[384,384]{1,0:T(8,128)S(1)} %dynamic-slice_bitcast_fusion.11), channel_id=1, source_target_pairs={{0,8},{4,12},{8,0},{12,4},{16,24},{20,28},{24,16},{28,20},{1,9},{5... | collective-permute-start | bytes 1769480 | tf_op jit(solution)/shard_map/ppermute | solution.py:147
  307.9 26.6 %slice-start = ((s8[7471104]{0:T(1024)(128)(4,1)}), s8[4194304]{0:T(1024)(128)(4,1)S(1)}, s32[]{:S(2)}) async-start(s8[7471104]{0:T(1024)(128)(4,1)} %bitcast.261), calls=%async_computation | async-start | bytes 8388608
  308.0 24.3 %collective-permute-start.35 = (f32[384,384]{1,0:T(8,128)S(1)}, f32[384,384]{1,0:T(8,128)S(1)}, u32[]{:S(2)}, u32[]{:S(2)}) collective-permute-start(f32[384,384]{1,0:T(8,128)S(1)} %dynamic-slice_bitcast_fusion.12), channel_id=1, source_target_pairs={{0,16},{4,20},{8,24},{12,28},{16,0},{20,4},{24,8},{28,12},{1,17},{... | collective-permute-start | bytes 1769480 | tf_op jit(solution)/shard_map/ppermute | solution.py:147
  320.5 19.2 %collective-permute-start.29 = (f32[48,3072]{1,0:T(8,128)S(1)}, f32[48,3072]{1,0:T(8,128)S(1)}, u32[]{:S(2)}, u32[]{:S(2)}) collective-permute-start(f32[48,3072]{1,0:T(8,128)S(1)} %dynamic-slice_bitcast_fusion.13), channel_id=1, source_target_pairs={{0,1},{1,0},{2,3},{3,2},{4,5},{5,4},{6,7},{7,6},{8,9},{9,8},{10,11... | collective-permute-start | bytes 1769480 | tf_op jit(solution)/shard_map/ppermute | solution.py:147
  332.5 21.4 %collective-permute-start.38 = (f32[192,768]{1,0:T(8,128)S(1)}, f32[192,768]{1,0:T(8,128)S(1)}, u32[]{:S(2)}, u32[]{:S(2)}) collective-permute-start(f32[192,768]{1,0:T(8,128)S(1)} %dynamic-slice_bitcast_fusion.10), channel_id=1, source_target_pairs={{0,1},{1,0},{2,3},{3,2},{4,5},{5,4},{6,7},{7,6},{8,9},{9,8},{10,11... | collective-permute-start | bytes 1769480 | tf_op jit(solution)/shard_map/ppermute | solution.py:147
  337.4 37.3 %collective-permute-start.7 = (f32[2,96,1152]{2,1,0:T(8,128)S(1)}, f32[2,96,1152]{2,1,0:T(8,128)S(1)}, u32[]{:S(2)}, u32[]{:S(2)}) collective-permute-start(f32[2,96,1152]{2,1,0:T(8,128)S(1)} %dynamic-slice_bitcast_fusion.9), channel_id=1, source_target_pairs={{0,8},{4,12},{8,0},{12,4},{16,24},{20,28},{24,16},{28,20},{1,9},{5... | collective-permute-start | bytes 2654216 | tf_op jit(solution)/shard_map/ppermute | solution.py:147
  339.3 42.7 %collective-permute-start.9 = (f32[2,96,1280]{2,1,0:T(8,128)S(1)}, f32[2,96,1280]{2,1,0:T(8,128)S(1)}, u32[]{:S(2)}, u32[]{:S(2)}) collective-permute-start(f32[2,96,1280]{2,1,0:T(8,128)S(1)} %dynamic-slice_bitcast_fusion.8), channel_id=1, source_target_pairs={{0,16},{4,20},{8,24},{12,28},{16,0},{20,4},{24,8},{28,12},{1,17},{... | collective-permute-start | bytes 2949128 | tf_op jit(solution)/shard_map/ppermute | solution.py:147
  339.7 14.3 %collective-permute-start.30 = (f32[24,3072]{1,0:T(8,128)S(1)}, f32[24,3072]{1,0:T(8,128)S(1)}, u32[]{:S(2)}, u32[]{:S(2)}) collective-permute-start(f32[24,3072]{1,0:T(8,128)S(1)} %dynamic-slice_bitcast_fusion.22), channel_id=1, source_target_pairs={{0,2},{1,3},{2,0},{3,1},{4,6},{5,7},{6,4},{7,5},{8,10},{9,11},{10,... | collective-permute-start | bytes 884744 | tf_op jit(solution)/shard_map/ppermute | solution.py:147
  354.0 20.6 %collective-permute-start.39 = (f32[96,768]{1,0:T(8,128)S(1)}, f32[96,768]{1,0:T(8,128)S(1)}, u32[]{:S(2)}, u32[]{:S(2)}) collective-permute-start(f32[96,768]{1,0:T(8,128)S(1)} %dynamic-slice_bitcast_fusion.21), channel_id=1, source_target_pairs={{0,2},{1,3},{2,0},{3,1},{4,6},{5,7},{6,4},{7,5},{8,10},{9,11},{10,... | collective-permute-start | bytes 884744 | tf_op jit(solution)/shard_map/ppermute | solution.py:147
  354.1 33.1 %collective-permute-start.31 = (f32[24,3072]{1,0:T(8,128)S(1)}, f32[24,3072]{1,0:T(8,128)S(1)}, u32[]{:S(2)}, u32[]{:S(2)}) collective-permute-start(f32[24,3072]{1,0:T(8,128)S(1)} %bitcast_add_fusion.23), channel_id=1, source_target_pairs={{0,2},{1,3},{2,0},{3,1},{4,6},{5,7},{6,4},{7,5},{8,10},{9,11},{10,... | collective-permute-start | bytes 884744 | tf_op jit(solution)/shard_map/ppermute | solution.py:147
  374.6 22.8 %collective-permute-start.40 = (f32[96,768]{1,0:T(8,128)S(1)}, f32[96,768]{1,0:T(8,128)S(1)}, u32[]{:S(2)}, u32[]{:S(2)}) collective-permute-start(f32[96,768]{1,0:T(8,128)S(1)} %bitcast_add_fusion.22), channel_id=1, source_target_pairs={{0,2},{1,3},{2,0},{3,1},{4,6},{5,7},{6,4},{7,5},{8,10},{9,11},{10,... | collective-permute-start | bytes 884744 | tf_op jit(solution)/shard_map/ppermute | solution.py:147
  374.8 17.4 %collective-permute-start.8 = (f32[96,1152]{1,0:T(8,128)S(1)}, f32[96,1152]{1,0:T(8,128)S(1)}, u32[]{:S(2)}, u32[]{:S(2)}) collective-permute-start(f32[96,1152]{1,0:T(8,128)S(1)} %dynamic-slice_bitcast_fusion.19), channel_id=1, source_target_pairs={{0,16},{4,20},{8,24},{12,28},{16,0},{20,4},{24,8},{28,12},{1,17},{... | collective-permute-start | bytes 1327112 | tf_op jit(solution)/shard_map/ppermute | solution.py:147
  382.2 12.8 %collective-permute-start.10 = (f32[96,1280]{1,0:T(8,128)S(1)}, f32[96,1280]{1,0:T(8,128)S(1)}, u32[]{:S(2)}, u32[]{:S(2)}) collective-permute-start(f32[96,1280]{1,0:T(8,128)S(1)} %dynamic-slice_bitcast_fusion.17), channel_id=1, source_target_pairs={{0,8},{4,12},{8,0},{12,4},{16,24},{20,28},{24,16},{28,20},{1,9},{5... | collective-permute-start | bytes 1474568 | tf_op jit(solution)/shard_map/ppermute | solution.py:147
  395.2 16.2 %collective-permute-start.11 = (f32[48,2432]{1,0:T(8,128)S(1)}, f32[48,2432]{1,0:T(8,128)S(1)}, u32[]{:S(2)}, u32[]{:S(2)}) collective-permute-start(f32[48,2432]{1,0:T(8,128)S(1)} %dynamic-slice_bitcast_fusion.18), channel_id=1, source_target_pairs={{0,1},{1,0},{2,3},{3,2},{4,5},{5,4},{6,7},{7,6},{8,9},{9,8},{10,11... | collective-permute-start | bytes 1400840 | tf_op jit(solution)/shard_map/ppermute | solution.py:147
  395.3 31.2 %collective-permute-start.32 = (f32[48,3072]{1,0:T(8,128)S(1)}, f32[48,3072]{1,0:T(8,128)S(1)}, u32[]{:S(2)}, u32[]{:S(2)}) collective-permute-start(f32[48,3072]{1,0:T(8,128)S(1)} %pad_maximum_fusion.12), channel_id=1, source_target_pairs={{0,1},{1,0},{2,3},{3,2},{4,5},{5,4},{6,7},{7,6},{8,9},{9,8},{10,11... | collective-permute-start | bytes 1769480 | tf_op jit(solution)/shard_map/ppermute | solution.py:147
  397.5 40.7 %collective-permute-start.41 = (f32[192,768]{1,0:T(8,128)S(1)}, f32[192,768]{1,0:T(8,128)S(1)}, u32[]{:S(2)}, u32[]{:S(2)}) collective-permute-start(f32[192,768]{1,0:T(8,128)S(1)} %pad_maximum_fusion.13), channel_id=1, source_target_pairs={{0,1},{1,0},{2,3},{3,2},{4,5},{5,4},{6,7},{7,6},{8,9},{9,8},{10,11... | collective-permute-start | bytes 1769480 | tf_op jit(solution)/shard_map/ppermute | solution.py:147
  411.4 23.2 %collective-permute-start.12 = (f32[24,2432]{1,0:T(8,128)S(1)}, f32[24,2432]{1,0:T(8,128)S(1)}, u32[]{:S(2)}, u32[]{:S(2)}) collective-permute-start(f32[24,2432]{1,0:T(8,128)S(1)} %dynamic-slice_bitcast_fusion.24), channel_id=1, source_target_pairs={{0,2},{1,3},{2,0},{3,1},{4,6},{5,7},{6,4},{7,5},{8,10},{9,11},{10,... | collective-permute-start | bytes 700424 | tf_op jit(solution)/shard_map/ppermute | solution.py:147
  434.7 13.9 %collective-permute-start.13 = (f32[24,2432]{1,0:T(8,128)S(1)}, f32[24,2432]{1,0:T(8,128)S(1)}, u32[]{:S(2)}, u32[]{:S(2)}) collective-permute-start(f32[24,2432]{1,0:T(8,128)S(1)} %bitcast_add_fusion.25), channel_id=1, source_target_pairs={{0,2},{1,3},{2,0},{3,1},{4,6},{5,7},{6,4},{7,5},{8,10},{9,11},{10,... | collective-permute-start | bytes 700424 | tf_op jit(solution)/shard_map/ppermute | solution.py:147
  448.7 11.8 %collective-permute-start.14 = (f32[48,2432]{1,0:T(8,128)S(1)}, f32[48,2432]{1,0:T(8,128)S(1)}, u32[]{:S(2)}, u32[]{:S(2)}) collective-permute-start(f32[48,2432]{1,0:T(8,128)S(1)} %pad_maximum_fusion.14), channel_id=1, source_target_pairs={{0,1},{1,0},{2,3},{3,2},{4,5},{5,4},{6,7},{7,6},{8,9},{9,8},{10,11... | collective-permute-start | bytes 1400840 | tf_op jit(solution)/shard_map/ppermute | solution.py:147
  (59 other events, 321.7 us)
